TPU v7x, 256 devices: a whole 4x4x8 slice. The times are simulated.
256 devices in a mesh: section: 8 (over z_hi, x), expert: 32 (over z_lo, y, core).
Axes of the slice: x: 4, y: 4, z: 8 (z_hi: 2, z_lo: 4; z = z_hi * 4 + z_lo), core: 2. Of those that a mesh axis runs over, the one named last changes fastest.
Arguments:
- forward_acts: bfloat16 [8, 4096, 2048], P('section', 'expert'), may hold values from -6 to 6
- forward_routes: int32 [8, 4096, 2], P('section', 'expert'), may hold values from 0 to 31, all different within a row; in each aligned block of 128 rows (0 to 127, 128 to 255, ..., all dimensions but the last counted through in order) at most 16 rows name the same one
- forward_gates: float32 [8, 4096, 2], P('section', 'expert'), may hold values from 0 to 1, as said below
- weight_in: bfloat16 [8, 32, 2048, 1536], P('section', 'expert'), may hold values from -0.125 to 0.125
- weight_down: bfloat16 [8, 32, 768, 2048], P('section', 'expert'), may hold values from -0.21875 to 0.21875
- saved_acts: bfloat16 [8, 4096, 2048], P('section', 'expert'), may hold values from -6 to 6
- backward_routes: int32 [8, 4096, 2], P('section', 'expert'), may hold values from 0 to 31, all different within a row; in each aligned block of 128 rows (0 to 127, 128 to 255, ..., all dimensions but the last counted through in order) at most 16 rows name the same one
- backward_gates: float32 [8, 4096, 2], P('section', 'expert'), may hold values from 0 to 1, as said below
- sent_grads: bfloat16 [8, 4096, 2048], P('section', 'expert'), may hold values from -6 to 6
Outputs:
- layer_out: bfloat16 [8, 4096, 2048], P('section', 'expert')
- input_grads: bfloat16 [8, 4096, 2048], P('section', 'expert')
Inputs may be any that keep to these rules, and one draw needn't show every extreme that they name: `forward_routes`: each row names 2 different experts. Among the entries of one section's tokens of one device (aligned blocks of 128 tokens) no expert is named more than 16 times, a bound that some block reaches. `backward_routes`: each row names 2 different experts. Among the entries of one section's tokens of one device (aligned blocks of 128 tokens) no expert is named more than 16 times, a bound that some block reaches. `forward_gates`: each row is positive and sums to 1. `backward_gates`: each row is positive and sums to 1.
All inputs are finite; a program needn't handle non-finite values.
Results may differ from a plain program's by a relative error of at most 0.008.
Values may be sent and summed in bfloat16 or wider, within the bound.
A program may use at most 64 MiB of HBM per device.

v0:
```python
import jax
import jax.numpy as jnp
from jax import lax
from jax.sharding import PartitionSpec as P


def extended(value, sides, width):
    for axis, dim in sides:
        devices, length = (lax.axis_size(axis), value.shape[dim])
        up = [(i, (i + 1) % devices) for i in range(devices)]
        down = [(j, i) for i, j in up]
        last = lax.slice_in_dim(value, length - width, length, axis=dim)
        first = lax.slice_in_dim(value, 0, width, axis=dim)
        before = lax.ppermute(last, axis, up)
        after = lax.ppermute(first, axis, down)
        value = jnp.concatenate([before, value, after], axis=dim)
    return value


def slot_index(routes, experts, capacity):
    labels = jnp.arange(experts, dtype=jnp.int32)
    onehot = (routes[:, None] == labels[None, :]).astype(jnp.int32)
    earlier = jnp.cumsum(onehot, axis=0) - onehot
    places = jnp.sum(earlier * onehot, axis=1)
    return routes * capacity + places


def expert_forward(rows, w_in, w_down):
    half = w_in.shape[1] // 2
    both = jnp.dot(rows, w_in, preferred_element_type=jnp.float32)
    gate_part = both[:, :half]
    up_part = both[:, half:]
    hidden = (gate_part * jax.nn.sigmoid(gate_part) * up_part).astype(jnp.bfloat16)
    return jnp.dot(hidden, w_down, preferred_element_type=jnp.float32).astype(jnp.bfloat16)


def expert_backward(rows, scaled_rows, w_in, w_down):
    half = w_in.shape[1] // 2
    both = jnp.dot(rows, w_in, preferred_element_type=jnp.float32)
    gate_part = both[:, :half]
    up_part = both[:, half:]
    sigma = jax.nn.sigmoid(gate_part)
    hidden_grad = lax.dot_general(
        scaled_rows, w_down, (((1,), (1,)), ((), ())), preferred_element_type=jnp.float32
    )
    gate_grad = hidden_grad * up_part * sigma * (1.0 + gate_part * (1.0 - sigma))
    up_grad = hidden_grad * gate_part * sigma
    joined = jnp.concatenate([gate_grad, up_grad], axis=1).astype(jnp.bfloat16)
    return lax.dot_general(
        joined, w_in, (((1,), (1,)), ((), ())), preferred_element_type=jnp.float32
    ).astype(jnp.bfloat16)


def per_device(
    forward_acts,
    forward_routes,
    forward_gates,
    weight_in,
    weight_down,
    saved_acts,
    backward_routes,
    backward_gates,
    sent_grads,
):
    stacked = jnp.concatenate([sent_grads, forward_acts], axis=0)
    widened = extended(stacked, (("section", 0),), 1)
    arriving = widened[0]
    incoming = widened[3]
    experts = lax.axis_size("expert")
    tokens_here = arriving.shape[0]
    width = arriving.shape[1]
    topk = forward_routes.shape[2]
    capacity = 2 * tokens_here * topk // experts
    w_in = weight_in[0, 0]
    w_down = weight_down[0, 0]
    forward_slots = slot_index(forward_routes[0].reshape(-1), experts, capacity)
    backward_slots = slot_index(backward_routes[0].reshape(-1), experts, capacity)

    def packed(rows, slots):
        empty = jnp.zeros((experts * capacity, width), jnp.bfloat16)
        return empty.at[slots].set(rows).reshape(experts, capacity, width)

    forward_send = packed(jnp.repeat(arriving, topk, axis=0), forward_slots)
    scaled = (backward_gates[0][:, :, None] * incoming.astype(jnp.float32)[:, None, :]).astype(
        jnp.bfloat16
    )
    backward_acts = packed(jnp.repeat(saved_acts[0], topk, axis=0), backward_slots)
    backward_grads = packed(scaled.reshape(-1, width), backward_slots)
    received = lax.all_to_all(forward_send, "expert", split_axis=0, concat_axis=0, tiled=True)
    count = received.shape[1]
    out_rows = expert_forward(received.reshape(-1, width), w_in, w_down).reshape(
        experts, count, width
    )
    forward_back = lax.all_to_all(out_rows, "expert", split_axis=0, concat_axis=0, tiled=True)
    acts_rows = lax.all_to_all(backward_acts, "expert", split_axis=0, concat_axis=0, tiled=True)
    grad_rows = lax.all_to_all(backward_grads, "expert", split_axis=0, concat_axis=0, tiled=True)
    count = acts_rows.shape[1]
    back_rows = expert_backward(
        acts_rows.reshape(-1, width), grad_rows.reshape(-1, width), w_in, w_down
    ).reshape(experts, count, width)
    backward_back = lax.all_to_all(back_rows, "expert", split_axis=0, concat_axis=0, tiled=True)
    forward_picked = forward_back.reshape(-1, width)[forward_slots].reshape(
        tokens_here, topk, width
    )
    mixed = arriving.astype(jnp.float32) + jnp.einsum(
        "tk,tkd->td", forward_gates[0], forward_picked.astype(jnp.float32)
    )
    backward_picked = backward_back.reshape(-1, width)[backward_slots].reshape(
        tokens_here, topk, width
    )
    total = incoming.astype(jnp.float32) + jnp.sum(backward_picked.astype(jnp.float32), axis=1)
    return (mixed.astype(jnp.bfloat16)[None], total.astype(jnp.bfloat16)[None])


def solution(mesh):
    placed = (
        P("section", "expert", None),
        P("section", "expert", None),
        P("section", "expert", None),
        P("section", "expert", None, None),
        P("section", "expert", None, None),
        P("section", "expert", None),
        P("section", "expert", None),
        P("section", "expert", None),
        P("section", "expert", None),
    )
    return jax.shard_map(
        per_device,
        mesh=mesh,
        in_specs=placed,
        out_specs=(P("section", "expert", None), P("section", "expert", None)),
        check_vma=False,
    )
```

profile of v0, /device:TPU:1, one launch (start us, length us, event | category | flops | bytes accessed | tf_op | source)
XLA Modules:
  0.0 360.8 jit_solution(18015777944804774823)
XLA Ops:
  0.6 0.0 copy-start
  0.6 0.9 copy.16
  1.6 0.1 eq.62
  1.7 0.1 eq.58
  1.9 0.7 broadcast_multiply_fusion
  2.6 0.6 reduce-window.16
  3.1 0.2 slice_reduce_fusion
  3.4 0.1 copy.15
  3.5 0.1 mul.80
  3.6 2.7 broadcast_in_dim.8
  6.3 2.3 reshape.202
  8.6 0.1 fusion.37
  8.7 4.4 %scatter_custom_fusion.2 = bf16[512,2048]{1,0:T(8,128)(2,1)} fusion(s32[256]{0:T(256)S(1)} %bitcast.98, bf16[256,2048]{1,0:T(8,128)(2,1)} %reshape.202, bf16[]{:T(256)} %constant.6.clone.1), kind=kCustom, calls=%fused_computation.36 | custom fusion | bytes 2097664 | tf_op jit(solution)/shard_map/scatter | solution.py:81
  13.1 10.4 %all-to-all-start.3 = ((bf16[32,16,2048]{2,1,0:T(8,128)(2,1)}), bf16[32,16,2048]{2,1,0:T(8,128)(2,1)}, u32[]{:S(2)}, u32[]{:S(2)}) async-start(bf16[32,16,2048]{2,1,0:T(8,128)(2,1)} %bitcast.93), calls=%async_computation.3 | async-start | bytes 4194304 | tf_op jit(solution)/shard_map/all_to_all | solution.py:95
  23.5 6.5 %collective-permute-start.1 = (bf16[1,128,2048]{2,1,0:T(8,128)(2,1)}, bf16[1,128,2048]{2,1,0:T(8,128)(2,1)}, u32[]{:S(2)}, u32[]{:S(2)}) collective-permute-start(bf16[1,128,2048]{2,1,0:T(8,128)(2,1)} %param.17), channel_id=1, source_target_pairs={{32,0},{64,32},{96,64},{128,96},{160,128},{192,160},{224,192},{0,2... | collective-permute-start | bytes 1572872 | tf_op jit(solution)/shard_map/ppermute | solution.py:15
  30.0 0.0 copy-done.3
  30.0 0.1 copy.19
  30.1 0.1 mul.82
  30.2 50.3 %collective-permute-done.1 = bf16[1,128,2048]{2,1,0:T(8,128)(2,1)} collective-permute-done((bf16[1,128,2048]{2,1,0:T(8,128)(2,1)}, bf16[1,128,2048]{2,1,0:T(8,128)(2,1)}, u32[]{:S(2)}, u32[]{:S(2)}) %collective-permute-start.1) | collective-permute-done | bytes 524320 | tf_op jit(solution)/shard_map/ppermute | solution.py:15
  80.5 1.1 convert_bitcast_fusion
  81.7 2.5 mul.84
  84.2 3.7 %mul.85 = f32[256,2048]{1,0:T(8,128)} reshape(f32[128,2,2048]{2,1,0:T(2,128)} %mul.84) | data formatting | bytes 4194304 | tf_op jit(solution)/shard_map/mul | solution.py:84
  87.8 4.8 %scatter_custom_fusion.1 = bf16[512,2048]{1,0:T(8,128)(2,1)} fusion(s32[256]{0:T(256)S(1)} %bitcast.99, f32[256,2048]{1,0:T(8,128)} %mul.85, f32[256]{0:T(256)S(1)} %mul.82, bf16[]{:T(256)} %constant.6.clone.1), kind=kCustom, calls=%fused_computation.32 | custom fusion | flops 1048576 | bytes 4195330 | tf_op jit(solution)/shard_map/scatter | solution.py:81
  92.7 1.4 all-to-all-done.3
  94.1 0.0 copy-start.2
  94.1 6.5 %all-to-all-start.2 = ((bf16[32,16,2048]{2,1,0:T(8,128)(2,1)}), bf16[32,16,2048]{2,1,0:T(8,128)(2,1)}, u32[]{:S(2)}, u32[]{:S(2)}) async-start(bf16[32,16,2048]{2,1,0:T(8,128)(2,1)} %bitcast.92), calls=%async_computation.2 | async-start | bytes 4194304 | tf_op jit(solution)/shard_map/all_to_all | solution.py:96
  100.7 0.3 collective-permute-start
  100.9 0.0 copy-done.2
  101.0 0.1 copy.12
  101.1 0.1 eq.54
  101.2 0.1 eq.50
  101.4 0.6 reduce-window.14
  102.0 0.2 slice_reduce_fusion.1
  102.2 0.1 copy.11
  102.3 0.1 mul.75
  102.5 0.1 fusion.40
  102.6 64.0 %collective-permute-done = bf16[1,128,2048]{2,1,0:T(8,128)(2,1)} collective-permute-done((bf16[1,128,2048]{2,1,0:T(8,128)(2,1)}, bf16[1,128,2048]{2,1,0:T(8,128)(2,1)}, u32[]{:S(2)}, u32[]{:S(2)}) %collective-permute-start) | collective-permute-done | bytes 524320 | tf_op jit(solution)/shard_map/ppermute | solution.py:14
  166.5 2.7 broadcast_in_dim.6
  169.2 2.3 reshape.186
  171.5 4.4 %scatter_custom_fusion = bf16[512,2048]{1,0:T(8,128)(2,1)} fusion(s32[256]{0:T(256)S(1)} %bitcast.101, bf16[256,2048]{1,0:T(8,128)(2,1)} %reshape.186, bf16[]{:T(256)} %constant.6.clone.1), kind=kCustom, calls=%fused_computation.39 | custom fusion | bytes 2097664 | tf_op jit(solution)/shard_map/scatter | solution.py:81
  175.9 0.0 all-to-all-done.2
  175.9 7.7 %all-to-all-start = ((bf16[32,16,2048]{2,1,0:T(8,128)(2,1)}), bf16[32,16,2048]{2,1,0:T(8,128)(2,1)}, u32[]{:S(2)}, u32[]{:S(2)}) async-start(bf16[32,16,2048]{2,1,0:T(8,128)(2,1)} %bitcast.94), calls=%async_computation | async-start | bytes 4194304 | tf_op jit(solution)/shard_map/all_to_all | solution.py:89
  183.6 6.2 %fusion.2 = f32[512,1536]{1,0:T(8,128)S(1)} fusion(bf16[512,2048]{1,0:T(8,128)(2,1)} %bitcast.22, bf16[1,1,2048,1536]{3,2,1,0:T(8,128)(2,1)} %param.12), kind=kOutput, calls=%fused_computation.7 | convolution fusion | flops 3221225472 | bytes 11534336 | tf_op jit(solution)/shard_map/dot_general | solution.py:39
  189.8 0.0 copy-done
  189.8 3.8 %fusion.18 = (bf16[512,768]{1,0:T(8,128)(2,1)S(1)}, bf16[512,768]{1,0:T(8,128)(2,1)S(1)}) fusion(f32[512,1536]{1,0:T(8,128)S(1)} %fusion.2, bf16[512,2048]{1,0:T(8,128)(2,1)} %bitcast.19, bf16[1,1,768,2048]{3,2,1,0:T(8,128)(2,1)S(1)} %copy-done), kind=kOutput, calls=%fused_computation.21 | convolution fusion | flops 1615724544 | bytes 9961472 | tf_op jit(solution)/shard_map/dot_general | solution.py:43
  193.6 7.4 %fusion.13 = bf16[512,2048]{1,0:T(8,128)(2,1)} fusion(bf16[1,1,2048,1536]{3,2,1,0:T(8,128)(2,1)} %param.12, bf16[512,768]{1,0:T(8,128)(2,1)S(1)} %get-tuple-element.3, bf16[512,768]{1,0:T(8,128)(2,1)S(1)} %get-tuple-element.2), kind=kOutput, calls=%fused_computation.16 | convolution fusion | flops 3225419776 | bytes 9961472 | tf_op jit(solution)/shard_map/dot_general | solution.py:49
  201.1 30.8 %all-to-all-done = bf16[32,16,2048]{2,1,0:T(8,128)(2,1)} async-done(((bf16[32,16,2048]{2,1,0:T(8,128)(2,1)}), bf16[32,16,2048]{2,1,0:T(8,128)(2,1)}, u32[]{:S(2)}, u32[]{:S(2)}) %all-to-all-start) | async-done | bytes 2097184 | tf_op jit(solution)/shard_map/all_to_all | solution.py:89
  231.8 6.4 %all-to-all-start.4 = ((bf16[32,16,2048]{2,1,0:T(8,128)(2,1)}), bf16[32,16,2048]{2,1,0:T(8,128)(2,1)}, u32[]{:S(2)}, u32[]{:S(2)}) async-start(bf16[32,16,2048]{2,1,0:T(8,128)(2,1)} %bitcast.96), calls=%async_computation.4 | async-start | bytes 4194304 | tf_op jit(solution)/shard_map/all_to_all | solution.py:101
  238.2 6.2 %fusion.4 = f32[512,1536]{1,0:T(8,128)S(1)} fusion(bf16[512,2048]{1,0:T(8,128)(2,1)} %bitcast.5, bf16[1,1,2048,1536]{3,2,1,0:T(8,128)(2,1)} %param.12), kind=kOutput, calls=%fused_computation.9 | convolution fusion | flops 3221225472 | bytes 11534336 | tf_op jit(solution)/shard_map/dot_general | solution.py:30
  244.4 3.2 fusion.10
  247.6 38.8 %all-to-all-done.4 = bf16[32,16,2048]{2,1,0:T(8,128)(2,1)} async-done(((bf16[32,16,2048]{2,1,0:T(8,128)(2,1)}), bf16[32,16,2048]{2,1,0:T(8,128)(2,1)}, u32[]{:S(2)}, u32[]{:S(2)}) %all-to-all-start.4) | async-done | bytes 2097184 | tf_op jit(solution)/shard_map/all_to_all | solution.py:101
  286.4 6.5 %all-to-all-start.1 = ((bf16[32,16,2048]{2,1,0:T(8,128)(2,1)}), bf16[32,16,2048]{2,1,0:T(8,128)(2,1)}, u32[]{:S(2)}, u32[]{:S(2)}) async-start(bf16[32,16,2048]{2,1,0:T(8,128)(2,1)} %bitcast.95), calls=%async_computation.1 | async-start | bytes 4194304 | tf_op jit(solution)/shard_map/all_to_all | solution.py:94
  293.0 0.0 copy-done.4
  293.0 0.2 copy.20
  293.2 5.2 %gather_fusion.1 = bf16[256,2048]{1,0:T(8,128)(2,1)} fusion(bf16[512,2048]{1,0:T(8,128)(2,1)} %bitcast.24, s32[1024]{0:T(1024)S(1)} %pad_clamp_fusion), kind=kCustom, calls=%fused_computation.1 | custom fusion | bytes 2098176 | tf_op jit(solution)/shard_map/gather | solution.py:108
  298.4 3.4 reshape.165
  301.8 39.4 %all-to-all-done.1 = bf16[32,16,2048]{2,1,0:T(8,128)(2,1)} async-done(((bf16[32,16,2048]{2,1,0:T(8,128)(2,1)}), bf16[32,16,2048]{2,1,0:T(8,128)(2,1)}, u32[]{:S(2)}, u32[]{:S(2)}) %all-to-all-start.1) | async-done | bytes 2097184 | tf_op jit(solution)/shard_map/all_to_all | solution.py:94
  341.2 5.2 %gather_fusion = bf16[256,2048]{1,0:T(8,128)(2,1)} fusion(bf16[512,2048]{1,0:T(8,128)(2,1)} %bitcast.9, s32[1024]{0:T(1024)S(1)} %pad_clamp_fusion.1), kind=kCustom, calls=%fused_computation | custom fusion | bytes 2098176 | tf_op jit(solution)/shard_map/gather | solution.py:102
  346.4 2.5 reshape.155
  348.9 5.1 %reduce_sum.37 = f32[128,2048]{1,0:T(8,128)} reduce(f32[128,2,2048]{2,1,0:T(2,128)} %reshape.165, f32[]{:T(128)} %constant.18.clone.1), dimensions={1}, to_apply=%region_9.10 | reduce | flops 262144 | bytes 3145732 | tf_op jit(solution)/shard_map/reduce_sum | solution.py:111
  354.0 2.5 fusion.45
  356.6 0.0 copy-done.1
  356.6 2.0 fusion.23
  358.5 2.2 fusion.34
  (14 shorter events, 0.1 us)
Async XLA Ops:
  0.6 189.2 %copy-start = (bf16[1,1,768,2048]{3,2,1,0:T(8,128)(2,1)S(1)}, bf16[1,1,768,2048]{3,2,1,0:T(8,128)(2,1)}, u32[]{:S(2)}) copy-start(bf16[1,1,768,2048]{3,2,1,0:T(8,128)(2,1)} %param.13) | copy-start | bytes 9437188
  13.1 16.9 %copy-start.3 = (f32[1,128,2]{1,2,0:T(2,128)S(1)}, f32[1,128,2]{1,2,0:T(2,128)}, u32[]{:S(2)}) copy-start(f32[1,128,2]{1,2,0:T(2,128)} %param.16) | copy-start | bytes 3076
  13.1 81.0 %all-to-all-start.3 = ((bf16[32,16,2048]{2,1,0:T(8,128)(2,1)}), bf16[32,16,2048]{2,1,0:T(8,128)(2,1)}, u32[]{:S(2)}, u32[]{:S(2)}) async-start(bf16[32,16,2048]{2,1,0:T(8,128)(2,1)} %bitcast.93), calls=%async_computation.3 | async-start | bytes 4194304 | tf_op jit(solution)/shard_map/all_to_all | solution.py:95
  23.5 57.1 %collective-permute-start.1 = (bf16[1,128,2048]{2,1,0:T(8,128)(2,1)}, bf16[1,128,2048]{2,1,0:T(8,128)(2,1)}, u32[]{:S(2)}, u32[]{:S(2)}) collective-permute-start(bf16[1,128,2048]{2,1,0:T(8,128)(2,1)} %param.17), channel_id=1, source_target_pairs={{32,0},{64,32},{96,64},{128,96},{160,128},{192,160},{224,192},{0,2... | collective-permute-start | bytes 1572872 | tf_op jit(solution)/shard_map/ppermute | solution.py:15
  94.1 6.8 %copy-start.2 = (s32[1,128,2]{1,2,0:T(2,128)S(1)}, s32[1,128,2]{1,2,0:T(2,128)}, u32[]{:S(2)}) copy-start(s32[1,128,2]{1,2,0:T(2,128)} %param.10) | copy-start | bytes 3076
  94.1 81.8 %all-to-all-start.2 = ((bf16[32,16,2048]{2,1,0:T(8,128)(2,1)}), bf16[32,16,2048]{2,1,0:T(8,128)(2,1)}, u32[]{:S(2)}, u32[]{:S(2)}) async-start(bf16[32,16,2048]{2,1,0:T(8,128)(2,1)} %bitcast.92), calls=%async_computation.2 | async-start | bytes 4194304 | tf_op jit(solution)/shard_map/all_to_all | solution.py:96
  100.7 65.8 %collective-permute-start = (bf16[1,128,2048]{2,1,0:T(8,128)(2,1)}, bf16[1,128,2048]{2,1,0:T(8,128)(2,1)}, u32[]{:S(2)}, u32[]{:S(2)}) collective-permute-start(bf16[1,128,2048]{2,1,0:T(8,128)(2,1)} %param.9), channel_id=1, source_target_pairs={{0,32},{32,64},{64,96},{96,128},{128,160},{160,192},{192,224},{224... | collective-permute-start | bytes 1572872 | tf_op jit(solution)/shard_map/ppermute | solution.py:14
  175.9 55.9 %all-to-all-start = ((bf16[32,16,2048]{2,1,0:T(8,128)(2,1)}), bf16[32,16,2048]{2,1,0:T(8,128)(2,1)}, u32[]{:S(2)}, u32[]{:S(2)}) async-start(bf16[32,16,2048]{2,1,0:T(8,128)(2,1)} %bitcast.94), calls=%async_computation | async-start | bytes 4194304 | tf_op jit(solution)/shard_map/all_to_all | solution.py:89
  231.8 54.6 %all-to-all-start.4 = ((bf16[32,16,2048]{2,1,0:T(8,128)(2,1)}), bf16[32,16,2048]{2,1,0:T(8,128)(2,1)}, u32[]{:S(2)}, u32[]{:S(2)}) async-start(bf16[32,16,2048]{2,1,0:T(8,128)(2,1)} %bitcast.96), calls=%async_computation.4 | async-start | bytes 4194304 | tf_op jit(solution)/shard_map/all_to_all | solution.py:101
  286.4 6.6 %copy-start.4 = (f32[1,128,2]{1,2,0:T(2,128)S(1)}, f32[1,128,2]{1,2,0:T(2,128)}, u32[]{:S(2)}) copy-start(f32[1,128,2]{1,2,0:T(2,128)} %param.11) | copy-start | bytes 3076
  286.4 54.7 %all-to-all-start.1 = ((bf16[32,16,2048]{2,1,0:T(8,128)(2,1)}), bf16[32,16,2048]{2,1,0:T(8,128)(2,1)}, u32[]{:S(2)}, u32[]{:S(2)}) async-start(bf16[32,16,2048]{2,1,0:T(8,128)(2,1)} %bitcast.95), calls=%async_computation.1 | async-start | bytes 4194304 | tf_op jit(solution)/shard_map/all_to_all | solution.py:94
  354.0 2.5 copy-start.1
where the time goes:
time: 362 us; the launch traced here: 361 us
  waiting for transfers between devices  225 us (62%)
  starting transfers between devices  44.3 us (12%)
  local copies, waits for them, and re-layouts  44.2 us (12%)
  matrix products  29.3 us (8%)
  other arithmetic  17.4 us (5%)
    ppermute x1, waiting for transfers between devices, extended(): before = lax.ppermute(last, axis, up)  64 us
    ppermute x1, waiting for transfers between devices, extended(): after = lax.ppermute(first, axis, down)  50.3 us
    all_to_all x1, waiting for transfers between devices, per_device(): lax.all_to_all(out_rows, 'expert', split_axis=0, concat_axis=0, tiled=True)  39.4 us
    all_to_all x1, waiting for transfers between devices, per_device(): lax.all_to_all(back_rows, 'expert', split_axis=0, concat_axis=0, tiled=True)  38.8 us
    all_to_all x1, waiting for transfers between devices, per_device(): lax.all_to_all(forward_send, 'expert', split_axis=0, concat_axis=0, tiled...  30.8 us
    all_to_all x1, starting transfers between devices, per_device(): lax.all_to_all(backward_acts, 'expert', split_axis=0, concat_axis=0, tile...  10.4 us
    scatter x2, local copies, waits for them, and re-layouts, packed(): return empty.at[slots].set(rows).reshape(experts, capacity, width)  8.8 us
    all_to_all x1, starting transfers between devices, per_device(): lax.all_to_all(forward_send, 'expert', split_axis=0, concat_axis=0, tiled...  7.69 us
  transfers between devices with their start and end apart: 7, of which 6 were waited for; matrix products, arithmetic and copies ran while one was open for 16% of the time, Pallas kernels for 0%

commit v1 on v0

v1 whole, which is shorter than its diff:
```python
import functools

import jax
import jax.numpy as jnp
from jax import lax
from jax.experimental import pallas as pl
from jax.experimental.pallas import tpu as pltpu
from jax.sharding import PartitionSpec as P

MESH = pl.DeviceIdType.MESH
F32 = jnp.float32
BF16 = jnp.bfloat16
D = 2048
FF = 768
TOK = 128
CAP = 16
PLANES = 4
PEERS = 8
EXPERTS = PLANES * PEERS

SAVED, GRAD, FWD = 0, 1, 2
BWD_OUT, FWD_OUT = 0, 1

DS, DG, DF, CB, CF, RB, RF, SF, FIN, META = range(10)
END_STEPS = (
    (DS, 0), (DG, 0), (META, 0), (DF, 0), (SF, 1), (CB, 0), (CF, 0), (DS, 1), (DG, 1), (CB, 1), (DS, 2), (RB, 1),
    (DG, 2), (CB, 2), (DS, 3), (RB, 2), (DG, 3), (CB, 3), (DF, 3), (RB, 3), (CF, 3), (DF, 2), (RF, 3), (CF, 2),
    (DF, 1), (RF, 2), (CF, 1), (FIN, 0), (RF, 1), (FIN, 1),
)
MID_STEPS = (
    (DS, 1), (DG, 1), (META, 0), (DS, 2), (DS, 0), (DF, 1), (DG, 2), (DG, 0), (CB, 1), (DS, 3), (DF, 0), (SF, 1),
    (CF, 1), (DG, 3), (CB, 2), (CB, 0), (DF, 3), (CB, 3), (DF, 2), (SF, 0), (CF, 0), (CF, 3), (RB, 2), (CF, 2),
    (RB, 3), (RB, 0), (RF, 3), (RF, 0), (RF, 2), (FIN, 0), (FIN, 1),
)


def lookup(step, steps):
    per = 5
    words = []
    for first in range(0, len(steps), per):
        part = steps[first : first + per]
        words.append(sum((op * 4 + block) * 64**i for i, (op, block) in enumerate(part)))
    word = jnp.int32(words[0])
    for i, w in enumerate(words[1:], 1):
        word = jnp.where(step // per == i, jnp.int32(w), word)
    place = lax.rem(step, per)
    scale = jnp.int32(1)
    for i in range(1, per):
        scale = jnp.where(place == i, jnp.int32(64**i), scale)
    return lax.rem(word // scale, 64)


def nt(a, b):
    return lax.dot_general(a, b, (((1,), (1,)), ((), ())), preferred_element_type=F32)


def nn(a, b):
    return jnp.dot(a, b, preferred_element_type=F32)


def kernel(
    meta_in, acts_in, saved_in, grads_in, w_in_hbm, w_down_hbm,
    out_f, out_b,
    gath, pk, rx, ou, rt, cin, ps, w_in, w_down, hid, joined, meta, meta_t,
    gath_sem, zs_sem, pks_sem, rx_sem, os_sem, rt_sem, cin_sem, ps_sem, meta_sem, ms_sem, w_sem, rl_sem,
):
    sec = lax.axis_index("section")
    me = lax.axis_index("expert")
    sections = lax.axis_size("section")
    z = me // PEERS
    lane = lax.rem(me, PEERS)
    ahead = lax.rem(sec + 1, sections)
    behind = lax.rem(sec + sections - 1, sections)
    flip = z >= 2
    is_mid = jnp.logical_and(z > 0, z < 3)

    def at_plane(plane):
        return (sec, plane * PEERS + lane)

    def at_peer(peer):
        return (sec, z * PEERS + peer)

    def rows(peer):
        return pl.ds(pl.multiple_of(peer * CAP, CAP), CAP)

    def remote(src, dst, send, recv, device):
        return pltpu.make_async_remote_copy(
            src_ref=src, dst_ref=dst, send_sem=send, recv_sem=recv, device_id=device, device_id_type=MESH
        )

    def wait_for(ref, sem):
        pltpu.make_async_copy(ref, ref, sem).wait()

    pltpu.make_async_copy(saved_in.at[0], gath.at[SAVED, z], gath_sem.at[SAVED, z]).start()
    load_in = pltpu.make_async_copy(w_in_hbm.at[0, 0], w_in, w_sem.at[0])
    load_down = pltpu.make_async_copy(w_down_hbm.at[0, 0], w_down, w_sem.at[1])
    load_in.start()
    load_down.start()

    barrier = pltpu.get_barrier_semaphore()
    for other in (ahead, behind):
        pl.semaphore_signal(barrier, inc=1, device_id=(other, me), device_id_type=MESH)
    for k in range(1, PLANES):
        pl.semaphore_signal(barrier, inc=1, device_id=at_plane(lax.rem(z + k, PLANES)), device_id_type=MESH)
    for k in range(1, PEERS):
        pl.semaphore_signal(barrier, inc=1, device_id=at_peer(lax.rem(lane + k, PEERS)), device_id_type=MESH)

    names = lax.broadcasted_iota(jnp.int32, (EXPERTS, TOK), 0).astype(F32)
    before = (
        lax.broadcasted_iota(jnp.int32, (TOK, TOK), 0) < lax.broadcasted_iota(jnp.int32, (TOK, TOK), 1)
    ).astype(F32).astype(BF16)
    table = meta_in[...]
    slots = []
    for first in (0, 2):
        hot = [(names == table[first + k : first + k + 1, :]).astype(F32) for k in range(2)]
        earlier = nn((hot[0] + hot[1]).astype(BF16), before)
        for k in range(2):
            place = jnp.sum(hot[k] * earlier, axis=0, keepdims=True)
            slots.append(table[first + k : first + k + 1, :] * float(CAP) + place)
    meta[z] = jnp.concatenate([*slots, table[4:8, :]], axis=0)

    pl.semaphore_wait(barrier, 2 + PLANES - 1 + PEERS - 1)

    relay_g = remote(grads_in.at[0], gath.at[GRAD, z], rl_sem.at[0], gath_sem.at[GRAD, z], (behind, me))
    relay_f = remote(acts_in.at[0], gath.at[FWD, z], rl_sem.at[1], gath_sem.at[FWD, z], (ahead, me))
    relay_g.start()
    relay_f.start()
    for k in range(1, PLANES):
        remote(meta.at[z], meta.at[z], ms_sem.at[k - 1], meta_sem.at[z], at_plane(lax.rem(z + k, PLANES))).start()

    def pass_on(t, b, right):
        return remote(
            gath.at[t, b],
            gath.at[t, b],
            zs_sem.at[t, b, 0 if right else 1],
            gath_sem.at[t, b],
            at_plane(z + 1 if right else z - 1),
        )

    def goes(b, right):
        return jnp.logical_and(b <= z, z < 3) if right else jnp.logical_and(b >= z, z > 0)

    def dispatch(t, b):
        wait_for(gath.at[t, b], gath_sem.at[t, b])
        for right in (True, False):
            cond = goes(b, right)
            if t == FWD:
                cond = jnp.logical_and(cond, b != z)

            @pl.when(cond)
            def _():
                pass_on(t, b, right).start()

        info = meta[b]
        first = 0 if t == FWD else 2
        wanted = (lax.broadcasted_iota(jnp.int32, (PEERS * CAP, TOK), 0) + z * (PEERS * CAP)).astype(F32)
        picks = [(wanted == info[first + k : first + k + 1, :]).astype(F32) for k in range(2)]
        pick = (picks[0] + picks[1]).astype(BF16)
        if t == GRAD:
            gate = jnp.sum(picks[0] * info[6:7, :] + picks[1] * info[7:8, :], axis=1, keepdims=True)
        for c in range(0, D, 512):
            part = nn(pick, gath[t, b, :, c : c + 512])
            if t == GRAD:
                part = part * gate
            pk[t, b, :, c : c + 512] = part.astype(BF16)
        for k in range(1, PEERS):
            peer = lax.rem(lane + k, PEERS)
            remote(
                pk.at[t, b, rows(peer)], rx.at[t, b, rows(lane)], pks_sem.at[t, b], rx_sem.at[t, b], at_peer(peer)
            ).start()
        pltpu.make_async_copy(pk.at[t, b, rows(lane)], rx.at[t, b, rows(lane)], rx_sem.at[t, b]).start()

    def give_back(x, b):
        for k in range(1, PEERS):
            peer = lax.rem(lane + k, PEERS)
            remote(
                ou.at[x, b, rows(peer)], rt.at[x, b, rows(lane)], os_sem.at[x, b], rt_sem.at[x, b], at_peer(peer)
            ).start()
        pltpu.make_async_copy(ou.at[x, b, rows(lane)], rt.at[x, b, rows(lane)], rt_sem.at[x, b]).start()

    def compute_forward(b):
        wait_for(rx.at[FWD, b], rx_sem.at[FWD, b])

        @pl.loop(0, FF // 256)
        def _(i):
            c = pl.multiple_of(i * 256, 256)
            x = rx[FWD, b]
            g = nn(x, w_in[:, pl.ds(c, 256)])
            u = nn(x, w_in[:, pl.ds(FF + c, 256)])
            hid[:, pl.ds(c, 256)] = (g * jax.nn.sigmoid(g) * u).astype(BF16)

        @pl.loop(0, D // 512)
        def _(i):
            c = pl.multiple_of(i * 512, 512)
            ou[FWD_OUT, b, :, pl.ds(c, 512)] = nn(hid[...], w_down[:, pl.ds(c, 512)]).astype(BF16)

        give_back(FWD_OUT, b)

    def compute_backward(b):
        wait_for(rx.at[SAVED, b], rx_sem.at[SAVED, b])
        wait_for(rx.at[GRAD, b], rx_sem.at[GRAD, b])

        @pl.loop(0, FF // 256)
        def _(i):
            c = pl.multiple_of(i * 256, 256)
            x = rx[SAVED, b]
            g = nn(x, w_in[:, pl.ds(c, 256)])
            u = nn(x, w_in[:, pl.ds(FF + c, 256)])
            h = nt(rx[GRAD, b], w_down[pl.ds(c, 256), :])
            s = jax.nn.sigmoid(g)
            joined[:, pl.ds(c, 256)] = (h * u * s * (1.0 + g * (1.0 - s))).astype(BF16)
            joined[:, pl.ds(FF + c, 256)] = (h * g * s).astype(BF16)

        @pl.loop(0, D // 256)
        def _(i):
            c = pl.multiple_of(i * 256, 256)
            ou[BWD_OUT, b, :, pl.ds(c, 256)] = nt(joined[...], w_in[pl.ds(c, 256), :]).astype(BF16)

        give_back(BWD_OUT, b)

    def weights_of(x, b):
        info = meta_t[b]
        wanted = (lax.broadcasted_iota(jnp.int32, (TOK, PEERS * CAP), 1) + z * (PEERS * CAP)).astype(F32)
        first = 0 if x == FWD_OUT else 2
        picks = [(wanted == info[:, first + k : first + k + 1]).astype(F32) for k in range(2)]
        if x == BWD_OUT:
            return [(picks[0] + picks[1]).astype(BF16)]
        full = picks[0] * info[:, 4:5] + picks[1] * info[:, 5:6]
        high = full.astype(BF16)
        return [high, (full - high.astype(F32)).astype(BF16)]

    def summed(x, b, weights, c):
        value = rt[x, b, :, c : c + 512]
        total = nn(weights[0], value)
        for w in weights[1:]:
            total = total + nn(w, value)
        return total

    def chain_out(x, b):
        right = b > z
        plane = jnp.where(right, z + 1, z - 1)
        slot = jnp.where(jnp.logical_and(jnp.logical_not(right), plane == b), 4, b)
        return remote(ps.at[x, b], cin.at[x, slot], ps_sem.at[x, b], cin_sem.at[x, slot], at_plane(plane))

    def reduce_step(x, b):
        wait_for(rt.at[x, b], rt_sem.at[x, b])
        weights = weights_of(x, b)
        has = is_mid

        @pl.when(has)
        def _():
            wait_for(cin.at[x, b], cin_sem.at[x, b])
            for c in range(0, D, 512):
                ps[x, b, :, c : c + 512] = (
                    summed(x, b, weights, c) + cin[x, b, :, c : c + 512].astype(F32)
                ).astype(BF16)

        @pl.when(jnp.logical_not(has))
        def _():
            for c in range(0, D, 512):
                ps[x, b, :, c : c + 512] = summed(x, b, weights, c).astype(BF16)

        chain_out(x, b).start()

    def finish(x):
        out = out_b if x == BWD_OUT else out_f
        t = GRAD if x == BWD_OUT else FWD
        wait_for(rt.at[x, z], rt_sem.at[x, z])
        weights = weights_of(x, z)

        @pl.when(z > 0)
        def _():
            wait_for(cin.at[x, z], cin_sem.at[x, z])

        @pl.when(z < 3)
        def _():
            wait_for(cin.at[x, 4], cin_sem.at[x, 4])

        for c in range(0, D, 512):
            total = gath[t, z, :, c : c + 512].astype(F32) + summed(x, z, weights, c)
            left = jnp.where(z > 0, cin[x, z, :, c : c + 512].astype(F32), 0.0)
            right = jnp.where(z < 3, cin[x, 4, :, c : c + 512].astype(F32), 0.0)
            out[0, :, c : c + 512] = (total + left + right).astype(BF16)

    def every_meta():
        for k in range(1, PLANES):
            b = lax.rem(z + k, PLANES)
            wait_for(meta.at[b], meta_sem.at[b])
        for b in range(PLANES):
            meta_t[b] = jnp.concatenate([meta[b]] * (TOK // 8), axis=0).T
        load_in.wait()
        load_down.wait()

    def own_forward(d):
        rightward = jnp.logical_xor(d == 1, flip)

        @pl.when(jnp.logical_and(rightward, z < 3))
        def _():
            pass_on(FWD, z, True).start()

        @pl.when(jnp.logical_and(jnp.logical_not(rightward), z > 0))
        def _():
            pass_on(FWD, z, False).start()

    n_steps = max(len(END_STEPS), len(MID_STEPS))
    n_mine = jnp.where(is_mid, len(MID_STEPS), len(END_STEPS))

    @pl.loop(0, n_steps)
    def _(i):
        code = jnp.where(is_mid, lookup(i, MID_STEPS), lookup(i, END_STEPS))
        code = jnp.where(i < n_mine, code, 63)
        op = code // 4
        raw = lax.rem(code, 4)
        b = jnp.where(flip, 3 - raw, raw)

        for number, run in (
            (DS, lambda: dispatch(SAVED, b)),
            (DG, lambda: dispatch(GRAD, b)),
            (DF, lambda: dispatch(FWD, b)),
            (CB, lambda: compute_backward(b)),
            (CF, lambda: compute_forward(b)),
            (RB, lambda: reduce_step(BWD_OUT, b)),
            (RF, lambda: reduce_step(FWD_OUT, b)),
            (SF, lambda: own_forward(raw)),
            (META, every_meta),
        ):
            pl.when(op == number)(run)
        pl.when(jnp.logical_and(op == FIN, raw == 0))(lambda: finish(BWD_OUT))
        pl.when(jnp.logical_and(op == FIN, raw == 1))(lambda: finish(FWD_OUT))

    relay_g.wait_send()
    relay_f.wait_send()
    for k in range(1, PLANES):
        remote(meta.at[z], meta.at[z], ms_sem.at[k - 1], meta_sem.at[z], at_plane(lax.rem(z + k, PLANES))).wait_send()
    sent = pl.ds(0, (PEERS - 1) * CAP)
    for b in range(PLANES):
        for t in range(3):
            for right in (True, False):

                @pl.when(goes(b, right))
                def _():
                    pass_on(t, b, right).wait_send()

            wait_for(pk.at[t, b, sent], pks_sem.at[t, b])
        for x in range(2):
            wait_for(ou.at[x, b, sent], os_sem.at[x, b])

            @pl.when(b != z)
            def _():
                wait_for(ps.at[x, b], ps_sem.at[x, b])


def per_device(acts, f_routes, f_gates, w_in, w_down, saved, b_routes, b_gates, grads):
    table = jnp.concatenate(
        [f_routes[0].T.astype(F32), b_routes[0].T.astype(F32), f_gates[0].T, b_gates[0].T], axis=0
    )
    dma = pltpu.SemaphoreType.DMA
    block = (TOK, D)
    out = jax.ShapeDtypeStruct((1, TOK, D), BF16)
    vmem = pl.BlockSpec(memory_space=pltpu.VMEM)
    hbm = pl.BlockSpec(memory_space=pl.ANY)
    return tuple(
        pl.pallas_call(
            kernel,
            name="moe_relay",
            out_shape=(out, out),
            in_specs=[vmem, hbm, hbm, hbm, hbm, hbm],
            out_specs=(vmem, vmem),
            scratch_shapes=[
                pltpu.VMEM((3, PLANES, *block), BF16),
                pltpu.VMEM((3, PLANES, *block), BF16),
                pltpu.VMEM((3, PLANES, *block), BF16),
                pltpu.VMEM((2, PLANES, *block), BF16),
                pltpu.VMEM((2, PLANES, *block), BF16),
                pltpu.VMEM((2, PLANES + 1, *block), BF16),
                pltpu.VMEM((2, PLANES, *block), BF16),
                pltpu.VMEM((D, 2 * FF), BF16),
                pltpu.VMEM((FF, D), BF16),
                pltpu.VMEM((TOK, FF), BF16),
                pltpu.VMEM((TOK, 2 * FF), BF16),
                pltpu.VMEM((PLANES, 8, TOK), F32),
                pltpu.VMEM((PLANES, TOK, TOK), F32),
                dma((3, PLANES)),
                dma((3, PLANES, 2)),
                dma((3, PLANES)),
                dma((3, PLANES)),
                dma((2, PLANES)),
                dma((2, PLANES)),
                dma((2, PLANES + 1)),
                dma((2, PLANES)),
                dma((PLANES,)),
                dma((PLANES - 1,)),
                dma((2,)),
                dma((2,)),
            ],
            compiler_params=pltpu.CompilerParams(
                collective_id=0, has_side_effects=True, vmem_limit_bytes=60 * 2**20
            ),
        )(table, acts, saved, grads, w_in, w_down)
    )


def solution(mesh):
    rows = P("section", "expert", None)
    weights = P("section", "expert", None, None)
    return jax.shard_map(
        per_device,
        mesh=mesh,
        in_specs=(rows, rows, rows, weights, weights, rows, rows, rows, rows),
        out_specs=(rows, rows),
        check_vma=False,
    )
```

time: 362 us -> 204 us (0.56)
  the two profiles are of different devices: /device:TPU:1 before, /device:TPU:167 now
where the time goes in v1:
time: 204 us; the launch traced here: 203 us
  Pallas kernels  197 us (97%)
  local copies, waits for them, and re-layouts  3.76 us (2%)
    pallas_call x1, Pallas kernels, per_device(): pl.pallas_call(kernel, name='moe_relay', out_shape=(out, out), in_specs=[...  197 us

profile of v1, /device:TPU:167, one launch (start us, length us, event | category | flops | bytes accessed | tf_op | source)
XLA Modules:
  0.0 203.3 jit_solution(14124116143007157199)
XLA Ops:
  0.6 0.7 convert_bitcast_fusion
  1.3 1.3 pad_maximum_fusion.meta_in
  2.6 196.9 %moe_relay.1 = (bf16[1,128,2048]{2,1,0:T(8,128)(2,1)}, bf16[1,128,2048]{2,1,0:T(8,128)(2,1)}) custom-call(f32[8,128]{1,0:T(8,128)} %pad_maximum_fusion.meta_in, bf16[1,128,2048]{2,1,0:T(8,128)(2,1)} %acts_in.1, bf16[1,128,2048]{2,1,0:T(8,128)(2,1)} %saved_in.1, bf16[1,128,2048]{2,1,0:T(8,128)(2,1)} %grads_in.1, bf16[1,1,2048,1536]{3,2,1,0:T(8,128)(2,1)} %w_in_hbm.1, ...), custom_call_target="tpu_custom_call" | custom-call | tf_op jit(solution)/shard_map/moe_relay/pallas_call | solution.py:363
  199.5 1.9 copy.13
  201.4 1.9 copy.14

commit v2 on v1

--- a/solution.py
+++ b/solution.py
@@ -21,28 +21,54 @@
 SAVED, GRAD, FWD = 0, 1, 2
 BWD_OUT, FWD_OUT = 0, 1
 
-DS, DG, DF, CB, CF, RB, RF, SF, FIN, META = range(10)
-END_STEPS = (
-    (DS, 0), (DG, 0), (META, 0), (DF, 0), (SF, 1), (CB, 0), (CF, 0), (DS, 1), (DG, 1), (CB, 1), (DS, 2), (RB, 1),
-    (DG, 2), (CB, 2), (DS, 3), (RB, 2), (DG, 3), (CB, 3), (DF, 3), (RB, 3), (CF, 3), (DF, 2), (RF, 3), (CF, 2),
-    (DF, 1), (RF, 2), (CF, 1), (FIN, 0), (RF, 1), (FIN, 1),
-)
-MID_STEPS = (
-    (DS, 1), (DG, 1), (META, 0), (DS, 2), (DS, 0), (DF, 1), (DG, 2), (DG, 0), (CB, 1), (DS, 3), (DF, 0), (SF, 1),
-    (CF, 1), (DG, 3), (CB, 2), (CB, 0), (DF, 3), (CB, 3), (DF, 2), (SF, 0), (CF, 0), (CF, 3), (RB, 2), (CF, 2),
-    (RB, 3), (RB, 0), (RF, 3), (RF, 0), (RF, 2), (FIN, 0), (FIN, 1),
-)
-
-
-def lookup(step, steps):
+TAKE, PACK, OWN, MAKE_B, MAKE_F, SUM_B, SUM_F, FINISH, TABLES, ACROSS, LAST = 0, 12, 24, 30, 34, 38, 42, 46, 48, 49, 51
+END_INNER = (
+    0, 48, 25, 4, 8, 16, 20, 27, 1, 12, 5, 17, 2, 29, 13, 14, 6, 18, 31, 32,
+    3, 7, 19, 15, 40, 11, 39, 23, 33, 28, 10, 37, 22, 41, 30, 45, 36, 9, 26, 24,
+    21, 44, 35, 43, 34, 47, 46,
+)
+MID_INNER = (
+    1, 25, 24, 48, 5, 26, 27, 13, 0, 17, 2, 4, 9, 6, 16, 3, 12, 31, 7, 8,
+    14, 20, 18, 30, 19, 15, 29, 11, 10, 23, 32, 28, 33, 40, 22, 34, 37, 41, 36, 45,
+    21, 38, 42, 44, 46, 35, 47,
+)
+END_FIRST = (
+    1, 0, 25, 4, 49, 48, 12, 16, 11, 23, 24, 37, 27, 5, 13, 50, 17, 2, 10, 14,
+    31, 3, 15, 6, 18, 45, 39, 7, 19, 32, 33, 40, 22, 8, 20, 41, 36, 9, 26, 21,
+    44, 35, 30, 43, 34, 47, 46,
+)
+MID_FIRST = (
+    1, 24, 25, 13, 5, 26, 27, 49, 17, 48, 31, 2, 0, 12, 3, 14, 11, 4, 6, 18,
+    16, 23, 7, 10, 15, 32, 19, 9, 37, 30, 8, 20, 33, 22, 45, 40, 34, 41, 21, 42,
+    36, 46, 38, 44, 35, 47,
+)
+END_LAST = (
+    48, 0, 25, 1, 8, 20, 12, 29, 49, 50, 7, 13, 19, 6, 2, 14, 18, 10, 22, 36,
+    3, 15, 28, 32, 44, 11, 34, 23, 33, 40, 5, 17, 41, 37, 31, 45, 9, 21, 24, 4,
+    16, 39, 35, 30, 43, 46, 47,
+)
+MID_LAST = (
+    1, 25, 24, 49, 9, 29, 0, 48, 12, 2, 14, 8, 10, 20, 22, 13, 3, 15, 34, 6,
+    11, 36, 23, 18, 5, 7, 19, 28, 4, 16, 17, 44, 32, 33, 31, 37, 41, 30, 45, 21,
+    38, 35, 42, 40, 47, 46,
+)
+
+
+def lookup(step, choices):
     per = 5
+    longest = max(len(steps) for _, steps in choices)
     words = []
-    for first in range(0, len(steps), per):
-        part = steps[first : first + per]
-        words.append(sum((op * 4 + block) * 64**i for i, (op, block) in enumerate(part)))
-    word = jnp.int32(words[0])
+    for first in range(0, longest, per):
+        word = None
+        for cond, steps in reversed(choices):
+            part = [*steps[first : first + per]]
+            part += [LAST] * (per - len(part))
+            here = jnp.int32(sum(number * 64**i for i, number in enumerate(part)))
+            word = here if word is None else jnp.where(cond, here, word)
+        words.append(word)
+    word = words[0]
     for i, w in enumerate(words[1:], 1):
-        word = jnp.where(step // per == i, jnp.int32(w), word)
+        word = jnp.where(step // per == i, w, word)
     place = lax.rem(step, per)
     scale = jnp.int32(1)
     for i in range(1, per):
@@ -61,18 +87,26 @@
 def kernel(
     meta_in, acts_in, saved_in, grads_in, w_in_hbm, w_down_hbm,
     out_f, out_b,
-    gath, pk, rx, ou, rt, cin, ps, w_in, w_down, hid, joined, meta, meta_t,
-    gath_sem, zs_sem, pks_sem, rx_sem, os_sem, rt_sem, cin_sem, ps_sem, meta_sem, ms_sem, w_sem, rl_sem,
+    gath, held, pk, rx, ou, rt, cin, ps, w_in, w_down, hid, joined, meta, meta_t,
+    gath_sem, held_sem, ac_sem, zs_sem, pks_sem, rx_sem, os_sem, rt_sem, cin_sem, ps_sem, meta_sem, ms_sem, w_sem, rl_sem,
 ):
     sec = lax.axis_index("section")
     me = lax.axis_index("expert")
-    sections = lax.axis_size("section")
     z = me // PEERS
     lane = lax.rem(me, PEERS)
-    ahead = lax.rem(sec + 1, sections)
-    behind = lax.rem(sec + sections - 1, sections)
+    half = sec // 4
+    x = lax.rem(sec, 4)
+    ahead = half * 4 + lax.rem(x + 1, 4)
+    behind = half * 4 + lax.rem(x + 3, 4)
+    first, last = x == 0, x == 3
+    crossing = jnp.logical_or(first, last)
+    across = (lax.rem(sec + 4, 8), (3 - z) * PEERS + lane)
     flip = z >= 2
     is_mid = jnp.logical_and(z > 0, z < 3)
+    is_end = jnp.logical_not(is_mid)
+
+    def crosses(t):
+        return jnp.logical_or(jnp.logical_and(t == FWD, first), jnp.logical_and(t == GRAD, last))
 
     def at_plane(plane):
         return (sec, plane * PEERS + lane)
@@ -105,26 +139,36 @@
     for k in range(1, PEERS):
         pl.semaphore_signal(barrier, inc=1, device_id=at_peer(lax.rem(lane + k, PEERS)), device_id_type=MESH)
 
+    @pl.when(jnp.logical_and(crossing, is_end))
+    def _():
+        pl.semaphore_signal(barrier, inc=1, device_id=across, device_id_type=MESH)
+
     names = lax.broadcasted_iota(jnp.int32, (EXPERTS, TOK), 0).astype(F32)
     before = (
         lax.broadcasted_iota(jnp.int32, (TOK, TOK), 0) < lax.broadcasted_iota(jnp.int32, (TOK, TOK), 1)
     ).astype(F32).astype(BF16)
     table = meta_in[...]
     slots = []
-    for first in (0, 2):
-        hot = [(names == table[first + k : first + k + 1, :]).astype(F32) for k in range(2)]
+    for row in (0, 2):
+        hot = [(names == table[row + k : row + k + 1, :]).astype(F32) for k in range(2)]
         earlier = nn((hot[0] + hot[1]).astype(BF16), before)
         for k in range(2):
             place = jnp.sum(hot[k] * earlier, axis=0, keepdims=True)
-            slots.append(table[first + k : first + k + 1, :] * float(CAP) + place)
+            slots.append(table[row + k : row + k + 1, :] * float(CAP) + place)
     meta[z] = jnp.concatenate([*slots, table[4:8, :]], axis=0)
 
-    pl.semaphore_wait(barrier, 2 + PLANES - 1 + PEERS - 1)
-
-    relay_g = remote(grads_in.at[0], gath.at[GRAD, z], rl_sem.at[0], gath_sem.at[GRAD, z], (behind, me))
-    relay_f = remote(acts_in.at[0], gath.at[FWD, z], rl_sem.at[1], gath_sem.at[FWD, z], (ahead, me))
-    relay_g.start()
-    relay_f.start()
+    partners = 2 + PLANES - 1 + PEERS - 1
+    pl.semaphore_wait(barrier, jnp.where(jnp.logical_and(crossing, is_end), partners + 1, partners))
+
+    def relay(t, to, stops, stop):
+        source = grads_in if t == GRAD else acts_in
+        number = 0 if t == GRAD else 1
+        target, sem = (held, held_sem) if stop else (gath.at[t], gath_sem.at[t])
+        return remote(source.at[0], target.at[z], rl_sem.at[number], sem.at[z], (to, me))
+
+    for t, to, stops in ((GRAD, behind, first), (FWD, ahead, last)):
+        pl.when(stops)(lambda: relay(t, to, stops, True).start())
+        pl.when(jnp.logical_not(stops))(lambda: relay(t, to, stops, False).start())
     for k in range(1, PLANES):
         remote(meta.at[z], meta.at[z], ms_sem.at[k - 1], meta_sem.at[z], at_plane(lax.rem(z + k, PLANES))).start()
 
@@ -137,32 +181,52 @@
             at_plane(z + 1 if right else z - 1),
         )
 
-    def goes(b, right):
-        return jnp.logical_and(b <= z, z < 3) if right else jnp.logical_and(b >= z, z > 0)
-
-    def dispatch(t, b):
+    def goes(t, b, right, own):
+        far = b >= 2 if right else b < 2
+        if own:
+            near = b <= z if right else b >= z
+        else:
+            near = b < z if right else b > z
+        there = z < 3 if right else z > 0
+        hot = crosses(t)
+        wanted = jnp.logical_or(jnp.logical_and(hot, far), jnp.logical_and(jnp.logical_not(hot), near))
+        return jnp.logical_and(wanted, there)
+
+    def take(t, b):
         wait_for(gath.at[t, b], gath_sem.at[t, b])
         for right in (True, False):
-            cond = goes(b, right)
-            if t == FWD:
-                cond = jnp.logical_and(cond, b != z)
-
-            @pl.when(cond)
-            def _():
-                pass_on(t, b, right).start()
-
+            pl.when(goes(t, b, right, False))(lambda: pass_on(t, b, right).start())
+
+    def own(t, d):
+        rightward = jnp.logical_xor(d == 1, flip)
+        pl.when(jnp.logical_and(rightward, z < 3))(lambda: pass_on(t, z, True).start())
+        pl.when(jnp.logical_and(jnp.logical_not(rightward), z > 0))(lambda: pass_on(t, z, False).start())
+
+    def held_on(b, k):
+        return remote(held.at[b], held.at[b], ac_sem.at[k], held_sem.at[b], at_plane(jnp.where(flip, z + 1, z - 1)))
+
+    def held_across(b, k):
+        t = jnp.where(first, FWD, GRAD)
+        return remote(held.at[b], gath.at[t, b], ac_sem.at[k], gath_sem.at[t, b], across)
+
+    def send_held(k):
+        b = jnp.where(k == 0, z, jnp.where(flip, 2, 1))
+        wait_for(held.at[b], held_sem.at[b])
+        pl.when(is_end)(lambda: held_across(b, k).start())
+        pl.when(is_mid)(lambda: held_on(b, k).start())
+
+    def pack(t, b):
         info = meta[b]
-        first = 0 if t == FWD else 2
         wanted = (lax.broadcasted_iota(jnp.int32, (PEERS * CAP, TOK), 0) + z * (PEERS * CAP)).astype(F32)
-        picks = [(wanted == info[first + k : first + k + 1, :]).astype(F32) for k in range(2)]
+        forward = t == FWD
+        picks = [
+            (wanted == jnp.where(forward, info[k : k + 1, :], info[2 + k : 3 + k, :])).astype(F32) for k in range(2)
+        ]
         pick = (picks[0] + picks[1]).astype(BF16)
-        if t == GRAD:
-            gate = jnp.sum(picks[0] * info[6:7, :] + picks[1] * info[7:8, :], axis=1, keepdims=True)
+        gate = jnp.sum(picks[0] * info[6:7, :] + picks[1] * info[7:8, :], axis=1, keepdims=True)
+        gate = jnp.where(t == GRAD, gate, 1.0)
         for c in range(0, D, 512):
-            part = nn(pick, gath[t, b, :, c : c + 512])
-            if t == GRAD:
-                part = part * gate
-            pk[t, b, :, c : c + 512] = part.astype(BF16)
+            pk[t, b, :, c : c + 512] = (nn(pick, gath[t, b, :, c : c + 512]) * gate).astype(BF16)
         for k in range(1, PEERS):
             peer = lax.rem(lane + k, PEERS)
             remote(
@@ -291,55 +355,44 @@
         load_in.wait()
         load_down.wait()
 
-    def own_forward(d):
-        rightward = jnp.logical_xor(d == 1, flip)
-
-        @pl.when(jnp.logical_and(rightward, z < 3))
-        def _():
-            pass_on(FWD, z, True).start()
-
-        @pl.when(jnp.logical_and(jnp.logical_not(rightward), z > 0))
-        def _():
-            pass_on(FWD, z, False).start()
-
-    n_steps = max(len(END_STEPS), len(MID_STEPS))
-    n_mine = jnp.where(is_mid, len(MID_STEPS), len(END_STEPS))
-
-    @pl.loop(0, n_steps)
+    end_tables = [(first, END_FIRST), (last, END_LAST), (None, END_INNER)]
+    mid_tables = [(first, MID_FIRST), (last, MID_LAST), (None, MID_INNER)]
+    choices = [(jnp.logical_and(is_mid, c) if c is not None else is_mid, steps) for c, steps in mid_tables]
+    choices += end_tables
+
+    def seen(raw):
+        return jnp.where(flip, 3 - raw, raw)
+
+    @pl.loop(0, max(len(steps) for _, steps in choices))
     def _(i):
-        code = jnp.where(is_mid, lookup(i, MID_STEPS), lookup(i, END_STEPS))
-        code = jnp.where(i < n_mine, code, 63)
-        op = code // 4
-        raw = lax.rem(code, 4)
-        b = jnp.where(flip, 3 - raw, raw)
-
-        for number, run in (
-            (DS, lambda: dispatch(SAVED, b)),
-            (DG, lambda: dispatch(GRAD, b)),
-            (DF, lambda: dispatch(FWD, b)),
-            (CB, lambda: compute_backward(b)),
-            (CF, lambda: compute_forward(b)),
-            (RB, lambda: reduce_step(BWD_OUT, b)),
-            (RF, lambda: reduce_step(FWD_OUT, b)),
-            (SF, lambda: own_forward(raw)),
-            (META, every_meta),
-        ):
-            pl.when(op == number)(run)
-        pl.when(jnp.logical_and(op == FIN, raw == 0))(lambda: finish(BWD_OUT))
-        pl.when(jnp.logical_and(op == FIN, raw == 1))(lambda: finish(FWD_OUT))
-
-    relay_g.wait_send()
-    relay_f.wait_send()
+        code = lookup(i, choices)
+
+        def during(start, end, run):
+            pl.when(jnp.logical_and(code >= start, code < end))(lambda: run(code - start))
+
+        during(TAKE, PACK, lambda n: take(n // 4, seen(lax.rem(n, 4))))
+        during(PACK, OWN, lambda n: pack(n // 4, seen(lax.rem(n, 4))))
+        during(OWN, MAKE_B, lambda n: own(n // 2, lax.rem(n, 2)))
+        during(MAKE_B, MAKE_F, lambda n: compute_backward(seen(n)))
+        during(MAKE_F, SUM_B, lambda n: compute_forward(seen(n)))
+        during(SUM_B, SUM_F, lambda n: reduce_step(BWD_OUT, seen(n)))
+        during(SUM_F, FINISH, lambda n: reduce_step(FWD_OUT, seen(n)))
+        during(FINISH, FINISH + 1, lambda n: finish(BWD_OUT))
+        during(FINISH + 1, TABLES, lambda n: finish(FWD_OUT))
+        during(TABLES, ACROSS, lambda n: every_meta())
+        during(ACROSS, LAST, send_held)
+
+    wait_for(held.at[z], rl_sem.at[0])
+    wait_for(held.at[z], rl_sem.at[1])
+    pl.when(crossing)(lambda: wait_for(held.at[z], ac_sem.at[0]))
+    pl.when(jnp.logical_and(crossing, is_end))(lambda: wait_for(held.at[z], ac_sem.at[1]))
     for k in range(1, PLANES):
         remote(meta.at[z], meta.at[z], ms_sem.at[k - 1], meta_sem.at[z], at_plane(lax.rem(z + k, PLANES))).wait_send()
     sent = pl.ds(0, (PEERS - 1) * CAP)
     for b in range(PLANES):
         for t in range(3):
             for right in (True, False):
-
-                @pl.when(goes(b, right))
-                def _():
-                    pass_on(t, b, right).wait_send()
+                pl.when(goes(t, b, right, True))(lambda: pass_on(t, b, right).wait_send())
 
             wait_for(pk.at[t, b, sent], pks_sem.at[t, b])
         for x in range(2):
@@ -368,6 +421,7 @@
             out_specs=(vmem, vmem),
             scratch_shapes=[
                 pltpu.VMEM((3, PLANES, *block), BF16),
+                pltpu.VMEM((PLANES, *block), BF16),
                 pltpu.VMEM((3, PLANES, *block), BF16),
                 pltpu.VMEM((3, PLANES, *block), BF16),
                 pltpu.VMEM((2, PLANES, *block), BF16),
@@ -381,6 +435,8 @@
                 pltpu.VMEM((PLANES, 8, TOK), F32),
                 pltpu.VMEM((PLANES, TOK, TOK), F32),
                 dma((3, PLANES)),
+                dma((PLANES,)),
+                dma((2,)),
                 dma((3, PLANES, 2)),
                 dma((3, PLANES)),
                 dma((3, PLANES)),

time: 204 us -> 167 us (0.82)
  the two profiles are of different devices: /device:TPU:167 before, /device:TPU:1 now
where the time goes in v2:
time: 167 us; the launch traced here: 165 us
  Pallas kernels  159 us (95%)
  local copies, waits for them, and re-layouts  3.76 us (2%)
  other arithmetic  2 us (1%)
    pallas_call x1, Pallas kernels, per_device(): pl.pallas_call(kernel, name='moe_relay', out_shape=(out, out), in_specs=[...  159 us
    unnamed x2, local copies, waits for them, and re-layouts  3.76 us

profile of v2, /device:TPU:1, one launch (start us, length us, event | category | flops | bytes accessed | tf_op | source)
XLA Modules:
  0.0 165.0 jit_solution(4132118533138078674)
XLA Ops:
  0.6 0.7 convert_bitcast_fusion
  1.3 1.3 pad_maximum_fusion.meta_in
  2.6 158.6 %moe_relay.1 = (bf16[1,128,2048]{2,1,0:T(8,128)(2,1)}, bf16[1,128,2048]{2,1,0:T(8,128)(2,1)}) custom-call(f32[8,128]{1,0:T(8,128)} %pad_maximum_fusion.meta_in, bf16[1,128,2048]{2,1,0:T(8,128)(2,1)} %acts_in.1, bf16[1,128,2048]{2,1,0:T(8,128)(2,1)} %saved_in.1, bf16[1,128,2048]{2,1,0:T(8,128)(2,1)} %grads_in.1, bf16[1,1,2048,1536]{3,2,1,0:T(8,128)(2,1)} %w_in_hbm.1, ...), custom_call_target="tpu_custom_call" | custom-call | tf_op jit(solution)/shard_map/moe_relay/pallas_call | solution.py:416
  161.3 1.9 %copy.13 = bf16[1,128,2048]{2,1,0:T(8,128)(2,1)} copy(bf16[1,128,2048]{2,1,0:T(8,128)(2,1)} %get-tuple-element.6) | data formatting | bytes 1048576
  163.2 1.9 %copy.14 = bf16[1,128,2048]{2,1,0:T(8,128)(2,1)} copy(bf16[1,128,2048]{2,1,0:T(8,128)(2,1)} %get-tuple-element.7) | data formatting | bytes 1048576

commit v3 on v2

--- a/solution.py
+++ b/solution.py
@@ -21,36 +21,34 @@
 SAVED, GRAD, FWD = 0, 1, 2
 BWD_OUT, FWD_OUT = 0, 1
 
-TAKE, PACK, OWN, MAKE_B, MAKE_F, SUM_B, SUM_F, FINISH, TABLES, ACROSS, LAST = 0, 12, 24, 30, 34, 38, 42, 46, 48, 49, 51
+TAKE, PACK, PACK_OUT, OWN, MAKE_B, MAKE_F = 0, 12, 24, 36, 39, 43
+SUM_B, SUM_F, FINISH, TABLES, ACROSS, LAST = 47, 51, 55, 57, 58, 60
 END_INNER = (
-    0, 48, 25, 4, 8, 16, 20, 27, 1, 12, 5, 17, 2, 29, 13, 14, 6, 18, 31, 32,
-    3, 7, 19, 15, 40, 11, 39, 23, 33, 28, 10, 37, 22, 41, 30, 45, 36, 9, 26, 24,
-    21, 44, 35, 43, 34, 47, 46,
+    0, 12, 36, 4, 8, 37, 57, 38, 20, 16, 40, 48, 41, 49, 42, 50, 46, 54, 45, 53,
+    44, 43, 39, 52, 55, 56,
 )
 MID_INNER = (
-    1, 25, 24, 48, 5, 26, 27, 13, 0, 17, 2, 4, 9, 6, 16, 3, 12, 31, 7, 8,
-    14, 20, 18, 30, 19, 15, 29, 11, 10, 23, 32, 28, 33, 40, 22, 34, 37, 41, 36, 45,
-    21, 38, 42, 44, 46, 35, 47,
+    1, 36, 25, 5, 29, 2, 37, 9, 57, 14, 21, 26, 0, 12, 17, 6, 30, 4, 3, 18,
+    15, 16, 27, 8, 7, 31, 19, 11, 20, 38, 23, 41, 35, 10, 42, 34, 22, 49, 46, 39,
+    33, 50, 13, 45, 54, 47, 43, 40, 53, 51, 44, 55, 56,
 )
 END_FIRST = (
-    1, 0, 25, 4, 49, 48, 12, 16, 11, 23, 24, 37, 27, 5, 13, 50, 17, 2, 10, 14,
-    31, 3, 15, 6, 18, 45, 39, 7, 19, 32, 33, 40, 22, 8, 20, 41, 36, 9, 26, 21,
-    44, 35, 30, 43, 34, 47, 46,
+    0, 57, 36, 12, 58, 4, 16, 37, 11, 23, 59, 46, 10, 22, 54, 41, 49, 45, 42, 53,
+    50, 40, 8, 20, 48, 44, 43, 39, 52, 56, 55,
 )
 MID_FIRST = (
-    1, 24, 25, 13, 5, 26, 27, 49, 17, 48, 31, 2, 0, 12, 3, 14, 11, 4, 6, 18,
-    16, 23, 7, 10, 15, 32, 19, 9, 37, 30, 8, 20, 33, 22, 45, 40, 34, 41, 21, 42,
-    36, 46, 38, 44, 35, 47,
+    1, 25, 36, 5, 37, 58, 17, 57, 13, 2, 14, 26, 0, 6, 18, 30, 4, 16, 3, 11,
+    15, 27, 23, 12, 7, 31, 19, 46, 10, 29, 22, 41, 8, 9, 20, 54, 21, 33, 42, 49,
+    43, 39, 50, 51, 45, 40, 53, 47, 44, 55, 56,
 )
 END_LAST = (
-    48, 0, 25, 1, 8, 20, 12, 29, 49, 50, 7, 13, 19, 6, 2, 14, 18, 10, 22, 36,
-    3, 15, 28, 32, 44, 11, 34, 23, 33, 40, 5, 17, 41, 37, 31, 45, 9, 21, 24, 4,
-    16, 39, 35, 30, 43, 46, 47,
+    0, 36, 58, 8, 20, 57, 38, 12, 7, 19, 59, 44, 6, 18, 52, 45, 42, 53, 50, 4,
+    46, 54, 41, 49, 16, 40, 39, 48, 43, 55, 56,
 )
 MID_LAST = (
-    1, 25, 24, 49, 9, 29, 0, 48, 12, 2, 14, 8, 10, 20, 22, 13, 3, 15, 34, 6,
-    11, 36, 23, 18, 5, 7, 19, 28, 4, 16, 17, 44, 32, 33, 31, 37, 41, 30, 45, 21,
-    38, 35, 42, 40, 47, 46,
+    1, 36, 25, 13, 58, 57, 2, 9, 38, 33, 14, 21, 10, 0, 22, 44, 34, 12, 7, 19,
+    3, 45, 27, 15, 8, 4, 16, 20, 11, 6, 23, 35, 42, 5, 26, 53, 18, 39, 29, 46,
+    50, 41, 43, 54, 47, 56, 17, 49, 51, 40, 55,
 )
 
 
@@ -87,8 +85,8 @@
 def kernel(
     meta_in, acts_in, saved_in, grads_in, w_in_hbm, w_down_hbm,
     out_f, out_b,
-    gath, held, pk, rx, ou, rt, cin, ps, w_in, w_down, hid, joined, meta, meta_t,
-    gath_sem, held_sem, ac_sem, zs_sem, pks_sem, rx_sem, os_sem, rt_sem, cin_sem, ps_sem, meta_sem, ms_sem, w_sem, rl_sem,
+    gath, held, pk, pk_out, rx, ou, rt, cin, ps, w_in, w_down, hid, joined, meta, meta_t,
+    gath_sem, held_sem, ac_sem, zs_sem, pks_sem, pko_sem, rx_sem, os_sem, rt_sem, cin_sem, ps_sem, meta_sem, ms_sem, w_sem, rl_sem,
 ):
     sec = lax.axis_index("section")
     me = lax.axis_index("expert")
@@ -131,13 +129,16 @@
     load_in.start()
     load_down.start()
 
+    pair = z + 1 - 2 * lax.rem(z, 2)
     barrier = pltpu.get_barrier_semaphore()
     for other in (ahead, behind):
         pl.semaphore_signal(barrier, inc=1, device_id=(other, me), device_id_type=MESH)
     for k in range(1, PLANES):
         pl.semaphore_signal(barrier, inc=1, device_id=at_plane(lax.rem(z + k, PLANES)), device_id_type=MESH)
     for k in range(1, PEERS):
-        pl.semaphore_signal(barrier, inc=1, device_id=at_peer(lax.rem(lane + k, PEERS)), device_id_type=MESH)
+        peer = lax.rem(lane + k, PEERS)
+        pl.semaphore_signal(barrier, inc=1, device_id=at_peer(peer), device_id_type=MESH)
+        pl.semaphore_signal(barrier, inc=1, device_id=(sec, pair * PEERS + peer), device_id_type=MESH)
 
     @pl.when(jnp.logical_and(crossing, is_end))
     def _():
@@ -157,7 +158,7 @@
             slots.append(table[row + k : row + k + 1, :] * float(CAP) + place)
     meta[z] = jnp.concatenate([*slots, table[4:8, :]], axis=0)
 
-    partners = 2 + PLANES - 1 + PEERS - 1
+    partners = 2 + PLANES - 1 + 2 * (PEERS - 1)
     pl.semaphore_wait(barrier, jnp.where(jnp.logical_and(crossing, is_end), partners + 1, partners))
 
     def relay(t, to, stops, stop):
@@ -182,25 +183,24 @@
         )
 
     def goes(t, b, right, own):
-        far = b >= 2 if right else b < 2
-        if own:
-            near = b <= z if right else b >= z
+        if right:
+            far, near, inner = b >= 2, (b <= z if own else b < z), z < 2
+            last_hop = jnp.logical_and(z == 2, b == 3)
         else:
-            near = b < z if right else b > z
-        there = z < 3 if right else z > 0
-        hot = crosses(t)
-        wanted = jnp.logical_or(jnp.logical_and(hot, far), jnp.logical_and(jnp.logical_not(hot), near))
-        return jnp.logical_and(wanted, there)
+            far, near, inner = b < 2, (b >= z if own else b > z), z > 1
+            last_hop = jnp.logical_and(z == 1, b == 0)
+        hot = jnp.logical_and(crosses(t), jnp.logical_and(far, jnp.logical_or(inner, last_hop)))
+        usual = jnp.logical_and(jnp.logical_not(crosses(t)), jnp.logical_and(near, inner))
+        return jnp.logical_or(hot, usual)
 
     def take(t, b):
         wait_for(gath.at[t, b], gath_sem.at[t, b])
         for right in (True, False):
             pl.when(goes(t, b, right, False))(lambda: pass_on(t, b, right).start())
 
-    def own(t, d):
-        rightward = jnp.logical_xor(d == 1, flip)
-        pl.when(jnp.logical_and(rightward, z < 3))(lambda: pass_on(t, z, True).start())
-        pl.when(jnp.logical_and(jnp.logical_not(rightward), z > 0))(lambda: pass_on(t, z, False).start())
+    def own(t):
+        pl.when(z < 2)(lambda: pass_on(t, z, True).start())
+        pl.when(z >= 2)(lambda: pass_on(t, z, False).start())
 
     def held_on(b, k):
         return remote(held.at[b], held.at[b], ac_sem.at[k], held_sem.at[b], at_plane(jnp.where(flip, z + 1, z - 1)))
@@ -215,9 +215,9 @@
         pl.when(is_end)(lambda: held_across(b, k).start())
         pl.when(is_mid)(lambda: held_on(b, k).start())
 
-    def pack(t, b):
+    def sort_rows(t, b, plane, target):
         info = meta[b]
-        wanted = (lax.broadcasted_iota(jnp.int32, (PEERS * CAP, TOK), 0) + z * (PEERS * CAP)).astype(F32)
+        wanted = (lax.broadcasted_iota(jnp.int32, (PEERS * CAP, TOK), 0) + plane * (PEERS * CAP)).astype(F32)
         forward = t == FWD
         picks = [
             (wanted == jnp.where(forward, info[k : k + 1, :], info[2 + k : 3 + k, :])).astype(F32) for k in range(2)
@@ -226,13 +226,28 @@
         gate = jnp.sum(picks[0] * info[6:7, :] + picks[1] * info[7:8, :], axis=1, keepdims=True)
         gate = jnp.where(t == GRAD, gate, 1.0)
         for c in range(0, D, 512):
-            pk[t, b, :, c : c + 512] = (nn(pick, gath[t, b, :, c : c + 512]) * gate).astype(BF16)
+            target[t, b, :, c : c + 512] = (nn(pick, gath[t, b, :, c : c + 512]) * gate).astype(BF16)
+
+    def pack(t, b):
+        sort_rows(t, b, z, pk)
         for k in range(1, PEERS):
             peer = lax.rem(lane + k, PEERS)
             remote(
                 pk.at[t, b, rows(peer)], rx.at[t, b, rows(lane)], pks_sem.at[t, b], rx_sem.at[t, b], at_peer(peer)
             ).start()
         pltpu.make_async_copy(pk.at[t, b, rows(lane)], rx.at[t, b, rows(lane)], rx_sem.at[t, b]).start()
+
+    outer = jnp.where(flip, 3, 0)
+    inner = jnp.where(flip, 2, 1)
+
+    def pack_out(t, b):
+        sort_rows(t, b, outer, pk_out)
+        for k in range(PEERS):
+            peer = lax.rem(lane + k, PEERS)
+            remote(
+                pk_out.at[t, b, rows(peer)], rx.at[t, b, rows(lane)], pko_sem.at[t, b], rx_sem.at[t, b],
+                (sec, outer * PEERS + peer),
+            ).start()
 
     def give_back(x, b):
         for k in range(1, PEERS):
@@ -371,8 +386,9 @@
             pl.when(jnp.logical_and(code >= start, code < end))(lambda: run(code - start))
 
         during(TAKE, PACK, lambda n: take(n // 4, seen(lax.rem(n, 4))))
-        during(PACK, OWN, lambda n: pack(n // 4, seen(lax.rem(n, 4))))
-        during(OWN, MAKE_B, lambda n: own(n // 2, lax.rem(n, 2)))
+        during(PACK, PACK_OUT, lambda n: pack(n // 4, seen(lax.rem(n, 4))))
+        during(PACK_OUT, OWN, lambda n: pack_out(n // 4, seen(lax.rem(n, 4))))
+        during(OWN, MAKE_B, own)
         during(MAKE_B, MAKE_F, lambda n: compute_backward(seen(n)))
         during(MAKE_F, SUM_B, lambda n: compute_forward(seen(n)))
         during(SUM_B, SUM_F, lambda n: reduce_step(BWD_OUT, seen(n)))
@@ -394,13 +410,17 @@
             for right in (True, False):
                 pl.when(goes(t, b, right, True))(lambda: pass_on(t, b, right).wait_send())
 
-            wait_for(pk.at[t, b, sent], pks_sem.at[t, b])
+            whole = jnp.logical_or(jnp.logical_and(crosses(t), b != inner), jnp.logical_and(jnp.logical_not(crosses(t)), b == outer))
+            pl.when(jnp.logical_or(is_mid, whole))(lambda: wait_for(pk.at[t, b, sent], pks_sem.at[t, b]))
+
+            usual = jnp.logical_and(jnp.logical_not(crosses(t)), b != outer)
+            hot = jnp.logical_and(crosses(t), b == inner)
+            pl.when(jnp.logical_and(is_mid, jnp.logical_or(usual, hot)))(
+                lambda: wait_for(pk_out.at[t, b], pko_sem.at[t, b])
+            )
         for x in range(2):
             wait_for(ou.at[x, b, sent], os_sem.at[x, b])
-
-            @pl.when(b != z)
-            def _():
-                wait_for(ps.at[x, b], ps_sem.at[x, b])
+            pl.when(b != z)(lambda: wait_for(ps.at[x, b], ps_sem.at[x, b]))
 
 
 def per_device(acts, f_routes, f_gates, w_in, w_down, saved, b_routes, b_gates, grads):
@@ -424,6 +444,7 @@
                 pltpu.VMEM((PLANES, *block), BF16),
                 pltpu.VMEM((3, PLANES, *block), BF16),
                 pltpu.VMEM((3, PLANES, *block), BF16),
+                pltpu.VMEM((3, PLANES, *block), BF16),
                 pltpu.VMEM((2, PLANES, *block), BF16),
                 pltpu.VMEM((2, PLANES, *block), BF16),
                 pltpu.VMEM((2, PLANES + 1, *block), BF16),
@@ -440,6 +461,7 @@
                 dma((3, PLANES, 2)),
                 dma((3, PLANES)),
                 dma((3, PLANES)),
+                dma((3, PLANES)),
                 dma((2, PLANES)),
                 dma((2, PLANES)),
                 dma((2, PLANES + 1)),
@@ -450,7 +472,7 @@
                 dma((2,)),
             ],
             compiler_params=pltpu.CompilerParams(
-                collective_id=0, has_side_effects=True, vmem_limit_bytes=60 * 2**20
+                collective_id=0, has_side_effects=True, vmem_limit_bytes=62 * 2**20
             ),
         )(table, acts, saved, grads, w_in, w_down)
     )

time: 167 us -> 168 us (level)
  the two profiles are of different devices: /device:TPU:1 before, /device:TPU:2 now
where the time goes in v3:
time: 168 us
  Pallas kernels  162 us (96%)
  local copies, waits for them, and re-layouts  3.76 us (2%)
  other arithmetic  2 us (1%)
    pallas_call x1, Pallas kernels, per_device(): pl.pallas_call(kernel, name='moe_relay', out_shape=(out, out), in_specs=[...  162 us
    unnamed x2, local copies, waits for them, and re-layouts  3.76 us

profile of v3, /device:TPU:2, one launch (start us, length us, event | category | flops | bytes accessed | tf_op | source)
XLA Modules:
  0.0 168.0 jit_solution(4416162938306019995)
XLA Ops:
  0.6 0.7 convert_bitcast_fusion
  1.3 1.3 pad_maximum_fusion.meta_in
  2.6 161.6 %moe_relay.1 = (bf16[1,128,2048]{2,1,0:T(8,128)(2,1)}, bf16[1,128,2048]{2,1,0:T(8,128)(2,1)}) custom-call(f32[8,128]{1,0:T(8,128)} %pad_maximum_fusion.meta_in, bf16[1,128,2048]{2,1,0:T(8,128)(2,1)} %acts_in.1, bf16[1,128,2048]{2,1,0:T(8,128)(2,1)} %saved_in.1, bf16[1,128,2048]{2,1,0:T(8,128)(2,1)} %grads_in.1, bf16[1,1,2048,1536]{3,2,1,0:T(8,128)(2,1)} %w_in_hbm.1, ...), custom_call_target="tpu_custom_call" | custom-call | tf_op jit(solution)/shard_map/moe_relay/pallas_call | solution.py:436
  164.3 1.9 %copy.13 = bf16[1,128,2048]{2,1,0:T(8,128)(2,1)} copy(bf16[1,128,2048]{2,1,0:T(8,128)(2,1)} %get-tuple-element.6) | data formatting | bytes 1048576
  166.1 1.9 %copy.14 = bf16[1,128,2048]{2,1,0:T(8,128)(2,1)} copy(bf16[1,128,2048]{2,1,0:T(8,128)(2,1)} %get-tuple-element.7) | data formatting | bytes 1048576
